TPU v7x, 512 devices: a whole 4x4x16 slice. The times are simulated.
512 devices in a mesh: seq: 64 (over y, x, z_lo), head: 8 (over z_hi, core).
Axes of the slice: x: 4, y: 4, z: 16 (z_hi: 4, z_lo: 4; z = z_hi * 4 + z_lo), core: 2. Of those that a mesh axis runs over, the one named last changes fastest.
Arguments:
- queries: bfloat16 [16384, 5120], P('seq', 'head'), may hold values from -100 to 100
- keys: bfloat16 [16384, 5120], P('seq', 'head'), may hold values from -12 to 12
- values: bfloat16 [16384, 5120], P('seq', 'head'), may hold values from -6 to 6
- hidden: bfloat16 [16384, 5120], P('seq', 'head'), may hold values from -3 to 3
- cached: bfloat16 [16384, 5120], P('seq', 'head'), may hold values from -6 to 6
- active: int32 [16384], P('seq'), may hold values from 0 to 1, as said below
- w_out: bfloat16 [5120, 5120], P('head', 'seq'), may hold values from -0.078125 to 0.078125
Outputs:
- block_output: bfloat16 [16384, 5120], P('seq', 'head')
Inputs may be any that keep to these rules, and one draw needn't show every extreme that they name: `active`: exactly 704 ones in all; among the 256 tokens of one index of seq at most 32 ones, and that many on some of them.
All inputs are finite; a program needn't handle non-finite values.
Results may differ from a plain program's by a relative error of at most 0.0039.
Values may be sent and summed in bfloat16 or wider, within the bound.
A program may use at most 64 MiB of HBM per device.

v0:
```python
import jax
import jax.numpy as jnp
from jax import lax
from jax.sharding import PartitionSpec as P

HD = 128


def for_sending(value):

    def short(part):
        return part.astype(jnp.bfloat16) if part.dtype == jnp.float32 else part

    return jax.tree.map(short, value)


def local_partials(query_rows, keys, values):
    head_count = keys.shape[1] // HD
    inv_root = 1.0 / HD**0.5

    def one_head(head):
        start = head * HD
        q_head = lax.dynamic_slice_in_dim(query_rows, start, HD, 1)
        k_head = lax.dynamic_slice_in_dim(keys, start, HD, 1)
        v_head = lax.dynamic_slice_in_dim(values, start, HD, 1)
        scores = (
            lax.dot_general(
                q_head, k_head, (((1,), (1,)), ((), ())), preferred_element_type=jnp.float32
            )
            * inv_root
        )
        peak = jnp.max(scores, axis=1)
        expo = jnp.exp(scores - peak[:, None])
        total = jnp.sum(expo, axis=1)
        block_out = jnp.dot(expo.astype(jnp.bfloat16), v_head, preferred_element_type=jnp.float32)
        return ((block_out / total[:, None]).astype(jnp.bfloat16), peak, total)

    return lax.map(one_head, jnp.arange(head_count, dtype=jnp.int32))


def shards(queries, keys, values, hidden, cached, active, w_out):
    tok_dev, features = queries.shape
    head_count = features // HD
    devices = lax.axis_size("seq")
    capacity = tok_dev // 8
    act_rows = jnp.nonzero(active, size=capacity, fill_value=tok_dev)[0].astype(jnp.int32)
    safe_rows = jnp.minimum(act_rows, tok_dev - 1)
    own_queries = queries[safe_rows]
    gathered = lax.all_gather(own_queries, "seq", axis=0, tiled=True)
    block_out, block_peak, block_total = local_partials(gathered, keys, values)
    block_out = block_out.reshape(head_count, devices, capacity, HD)
    peak_in, total_in = (
        lax.all_to_all(
            block_peak.reshape(head_count, devices, capacity),
            "seq",
            split_axis=1,
            concat_axis=1,
            tiled=True,
        ),
        lax.all_to_all(
            block_total.reshape(head_count, devices, capacity),
            "seq",
            split_axis=1,
            concat_axis=1,
            tiled=True,
        ),
    )
    out_in = lax.all_to_all(
        for_sending(block_out), "seq", split_axis=1, concat_axis=1, tiled=True
    ).astype(block_out.dtype)
    top_max = jnp.max(peak_in, axis=1, keepdims=True)
    weight = total_in * jnp.exp(peak_in - top_max)
    mixed = jnp.einsum("hnc,hncd->hcd", weight, out_in.astype(jnp.float32))
    mixed = mixed / jnp.sum(weight, axis=1)[:, :, None]
    attn = jnp.transpose(mixed, (1, 0, 2)).reshape(capacity, features).astype(jnp.bfloat16)
    terms = jnp.dot(
        attn, lax.all_gather(w_out, "seq", axis=1, tiled=True), preferred_element_type=jnp.float32
    )
    summed = lax.psum_scatter(
        terms.astype(jnp.bfloat16), "head", scatter_dimension=1, tiled=True
    ).astype(jnp.float32)
    updated = (hidden[safe_rows].astype(jnp.float32) + summed).astype(jnp.bfloat16)
    return cached.at[act_rows].set(updated, mode="drop")


def solution(mesh):
    placed = (
        P("seq", "head"),
        P("seq", "head"),
        P("seq", "head"),
        P("seq", "head"),
        P("seq", "head"),
        P("seq"),
        P("head", "seq"),
    )
    return jax.shard_map(
        shards, mesh=mesh, in_specs=placed, out_specs=P("seq", "head"), check_vma=False
    )
```

profile of v0, /device:TPU:1, one launch (start us, length us, event | category | flops | bytes accessed | tf_op | source)
XLA Modules:
  0.0 835.7 jit_solution(14401901333159567819)
XLA Ops:
  6.5 1.8 copy.56
  9.0 1.4 fusion.25
  11.0 2.3 scatter_custom_fusion
  13.5 1.3 fusion.23
  14.8 2.3 gather_fusion
  17.9 318.7 %all-gather.6.cloned.1.call-done = bf16[2048,640]{1,0:T(8,128)(2,1)} async-done(((bf16[32,640]{1,0:T(8,128)(2,1)}), bf16[2048,640]{1,0:T(8,128)(2,1)}) %all-gather.6.cloned.1.call-update) | async-done | bytes 2621456 | tf_op jit(solution)/shard_map/all_gather | solution.py:49
  336.5 25.5 %while.14 = (s32[]{:T(128)}, bf16[5,2048,128]{2,1,0:T(8,128)(2,1)S(1)}, f32[5,2048]{1,0:T(8,128)S(1)}, f32[5,2048]{1,0:T(8,128)S(1)}, s32[5]{0:T(128)S(1)}, /*in...) while((s32[]{:T(128)}, ...), condition=%wide.region_8.9_spmd, body=%wide.region_5.8_spmd.sunk | while | flops 272101376 | bytes 7546555 | solution.py:38
  337.8 1.5 fusion.39
  339.6 1.6 fusion.41
  342.9 1.5 fusion.39
  344.7 1.6 fusion.41
  348.0 1.5 fusion.39
  349.8 1.6 fusion.41
  353.1 1.5 fusion.39
  354.9 1.6 fusion.41
  358.2 1.5 fusion.39
  360.0 1.6 fusion.41
  363.0 7.7 all-to-all-start.2
  371.7 7.9 all-to-all-done.2
  379.6 4.6 all-to-all-start.1
  384.2 2.0 copy.16
  386.2 6.8 all-to-all-done.1
  393.0 4.7 all-to-all-start
  400.7 1.4 fusion.16
  403.2 1.4 fusion.15
  405.3 55.5 %all-to-all-done = bf16[5,64,32,128]{3,2,0,1:T(8,128)(2,1)S(1)} async-done(((bf16[5,64,32,128]{3,2,0,1:T(8,128)(2,1)}), bf16[5,64,32,128]{3,2,0,1:T(8,128)(2,1)S(1)}, u32[]{:S(2)}, u32[]{:S(2)}) %all-to-all-start) | async-done | bytes 2621472 | tf_op jit(solution)/shard_map/all_to_all | solution.py:68
  460.8 1.4 fusion.12
  462.3 259.2 %all-gather.4.cloned.1.call-done = bf16[640,5120]{0,1:T(8,128)(2,1)} async-done(((bf16[640,80]{0,1:T(8,128)(2,1)}), bf16[640,5120]{0,1:T(8,128)(2,1)}) %all-gather.4.cloned.1.call-update) | async-done | bytes 6553616 | tf_op jit(solution)/shard_map/all_gather | solution.py:77
  721.5 4.9 convolution_convert_fusion
  726.5 1.4 copy.24
  727.9 97.5 %reduce-scatter.4.cloned.1.call-done = bf16[640,32]{1,0:T(8,128)(2,1)} async-done(((bf16[5120,32]{1,0:T(8,128)(2,1)}), bf16[640,32]{1,0:T(8,128)(2,1)}) %reduce-scatter.4.cloned.1.call-update) | async-done | bytes 40976
  826.5 2.7 scatter_custom_fusion.1
  (63 shorter events, 16.6 us)
Async XLA Ops:
  6.5 819.9 %copy-start = (bf16[256,640]{1,0:T(8,128)(2,1)S(1)}, bf16[256,640]{1,0:T(8,128)(2,1)}, u32[]{:S(2)}) copy-start(bf16[256,640]{1,0:T(8,128)(2,1)} %param.12) | copy-start | bytes 983044
  6.5 330.0 %all-gather.6.cloned.1.call-start = ((), (), s32[]{:S(2)}) async-start(), calls=%async_computation.5 | async-start | bytes 2662400 | tf_op jit(solution)/shard_map/all_gather | solution.py:49
  14.8 2.3 copy-start.1
  17.1 704.4 %all-gather.4.cloned.1.call-start = ((), (), s32[]{:S(2)}) async-start(), calls=%async_computation.4 | async-start | bytes 6656000 | tf_op jit(solution)/shard_map/all_gather | solution.py:77
  363.0 16.5 %all-to-all-start.2 = ((f32[64,1,160]{2,1,0:T(1,128)}), f32[64,1,160]{2,1,0:T(1,128)S(1)}, u32[]{:S(2)}, u32[]{:S(2)}) async-start(f32[64,1,160]{2,1,0:T(1,128)} %reshape.196), calls=%async_computation.2 | async-start | bytes 131072 | tf_op jit(solution)/shard_map/all_to_all | solution.py:53
  379.6 13.5 %all-to-all-start.1 = ((f32[64,1,160]{2,1,0:T(1,128)}), f32[64,1,160]{2,1,0:T(1,128)S(1)}, u32[]{:S(2)}, u32[]{:S(2)}) async-start(f32[64,1,160]{2,1,0:T(1,128)} %reshape.194), calls=%async_computation.1 | async-start | bytes 131072 | tf_op jit(solution)/shard_map/all_to_all | solution.py:60
  393.0 67.8 %all-to-all-start = ((bf16[5,64,32,128]{3,2,0,1:T(8,128)(2,1)}), bf16[5,64,32,128]{3,2,0,1:T(8,128)(2,1)S(1)}, u32[]{:S(2)}, u32[]{:S(2)}) async-start(bf16[5,64,32,128]{3,2,0,1:T(8,128)(2,1)} %copy.16), calls=%async_computation | async-start | bytes 5242880 | tf_op jit(solution)/shard_map/all_to_all | solution.py:68
  397.7 427.7 %reduce-scatter.4.cloned.1.call-start = ((), (), s32[]{:S(2)}) async-start(), calls=%async_computation.6 | async-start | bytes 1474560
  726.4 100.0 %copy-start.2 = (s32[1024]{0:T(1024)S(1)}, s32[1024]{0:T(1024)}, u32[]{:S(2)}) copy-start(s32[1024]{0:T(1024)} %copy-done.1) | copy-start | bytes 12292
Sparse Core Ops, SparseCore 0:
  17.2 319.2 all-gather.5
  338.6 382.8 all-gather.3
  728.0 97.3 reduce-scatter.3
where the time goes:
time: 837 us; the launch traced here: 836 us
  waiting for transfers between devices  746 us (89%)
  matrix products  21.9 us (3%)
  local copies, waits for them, and re-layouts  18.3 us (2%)
  starting transfers between devices  17.1 us (2%)
  other arithmetic  15.5 us (2%)
  between operations  13.3 us (2%)
    all_gather x1, waiting for transfers between devices, shards(): gathered = lax.all_gather(own_queries, 'seq', axis=0, tiled=True)  319 us
    all_gather x1, waiting for transfers between devices, shards(): lax.all_gather(w_out, 'seq', axis=1, tiled=True)  259 us
    unnamed x4, waiting for transfers between devices  98.2 us
    all_to_all x1, waiting for transfers between devices, shards(): lax.all_to_all(for_sending(block_out), 'seq', split_axis=1, concat_axis=1...  55.5 us
  transfers between devices with their start and end apart: 6, of which 6 were waited for; matrix products, arithmetic and copies ran while one was open for 4% of the time, Pallas kernels for 0%

commit v1 on v0

--- a/solution.py
+++ b/solution.py
@@ -39,6 +39,15 @@
 
 
 def shards(queries, keys, values, hidden, cached, active, w_out):
+
+    def _put_shards(vec):
+        return jnp.concatenate(
+            lax.all_to_all(
+                jnp.stack(tuple((vec for _ in range(lax.axis_size("seq"))))), "seq", 0, 0
+            ),
+            axis=1,
+        )
+
     tok_dev, features = queries.shape
     head_count = features // HD
     devices = lax.axis_size("seq")
@@ -73,9 +82,7 @@
     mixed = jnp.einsum("hnc,hncd->hcd", weight, out_in.astype(jnp.float32))
     mixed = mixed / jnp.sum(weight, axis=1)[:, :, None]
     attn = jnp.transpose(mixed, (1, 0, 2)).reshape(capacity, features).astype(jnp.bfloat16)
-    terms = jnp.dot(
-        attn, lax.all_gather(w_out, "seq", axis=1, tiled=True), preferred_element_type=jnp.float32
-    )
+    terms = jnp.dot(attn, _put_shards(w_out), preferred_element_type=jnp.float32)
     summed = lax.psum_scatter(
         terms.astype(jnp.bfloat16), "head", scatter_dimension=1, tiled=True
     ).astype(jnp.float32)

time: 837 us -> 697 us (0.83)
  waiting for transfers between devices: 746 us -> 560 us
  blocking collectives: 0 us -> 40.7 us
    all_gather x1 -> x0, waiting for transfers between devices: 259 us -> none  [shards(): lax.all_gather(w_out, 'seq', axis=1, tiled=True)]
    all_to_all x1, waiting for transfers between devices: 55.5 us -> 98.9 us  [_put_shards(): lax.all_to_all(jnp.stack(tuple((vec for _ in range(lax.axis_size('seq')))...]
    all_to_all x0 -> x1, blocking collectives: none -> 40.7 us  [shards(): lax.all_to_all(for_sending(block_out), 'seq', split_axis=1, concat_axis=1...]
    unnamed x4 -> x3, waiting for transfers between devices: 98.2 us -> 127 us
  transfers between devices with their start and end apart: 6 -> 5, of which waited for: 6 -> 5; matrix products, arithmetic and copies ran while one was open for 4% -> 2% of each run, Pallas kernels for 0% -> 0%
where the time goes in v1:
time: 697 us; the launch traced here: 695 us
  waiting for transfers between devices  560 us (80%)
  blocking collectives  40.7 us (6%)
  local copies, waits for them, and re-layouts  22 us (3%)
  matrix products  21.9 us (3%)
  starting transfers between devices  18.3 us (3%)
  other arithmetic  15.6 us (2%)
  between operations  13.6 us (2%)
    all_gather x1, waiting for transfers between devices, shards(): gathered = lax.all_gather(own_queries, 'seq', axis=0, tiled=True)  319 us
    unnamed x3, waiting for transfers between devices  127 us
    all_to_all x1, waiting for transfers between devices, _put_shards(): lax.all_to_all(jnp.stack(tuple((vec for _ in range(lax.axis_size('seq')))...  98.9 us
    all_to_all x1, blocking collectives, shards(): lax.all_to_all(for_sending(block_out), 'seq', split_axis=1, concat_axis=1...  40.7 us
  transfers between devices with their start and end apart: 5, of which 5 were waited for; matrix products, arithmetic and copies ran while one was open for 2% of the time, Pallas kernels for 0%

profile of v1, /device:TPU:1, one launch (start us, length us, event | category | flops | bytes accessed | tf_op | source)
XLA Modules:
  0.0 695.5 jit_solution(2094449420156169448)
XLA Ops:
  6.5 1.8 copy.57
  9.0 1.4 fusion.25
  11.0 2.3 scatter_custom_fusion
  14.8 2.3 gather_fusion
  17.1 319.4 %all-gather.3.cloned.1.call-done = bf16[2048,640]{1,0:T(8,128)(2,1)} async-done(((bf16[32,640]{1,0:T(8,128)(2,1)}), bf16[2048,640]{1,0:T(8,128)(2,1)}) %all-gather.3.cloned.1.call-update) | async-done | bytes 2621456 | tf_op jit(solution)/shard_map/all_gather | solution.py:58
  336.6 25.7 %while.14 = (s32[]{:T(128)}, bf16[5,2048,128]{2,1,0:T(8,128)(2,1)S(1)}, f32[5,2048]{1,0:T(8,128)S(1)}, f32[5,2048]{1,0:T(8,128)S(1)}, s32[5]{0:T(128)S(1)}, /*in...) while((s32[]{:T(128)}, ...), condition=%wide.region_8.9_spmd, body=%wide.region_5.8_spmd.sunk | while | flops 272101376 | bytes 7546555 | solution.py:38
  337.8 1.5 fusion.39
  339.6 1.6 fusion.41
  342.9 1.5 fusion.39
  344.8 1.6 fusion.41
  348.1 1.5 fusion.39
  349.9 1.6 fusion.41
  353.2 1.5 fusion.39
  355.0 1.6 fusion.41
  358.4 1.5 fusion.39
  360.2 1.6 fusion.41
  363.5 7.6 %all-to-all-start.2 = ((f32[64,1,160]{2,1,0:T(1,128)}), f32[64,1,160]{2,1,0:T(1,128)S(1)}, u32[]{:S(2)}, u32[]{:S(2)}) async-start(f32[64,1,160]{2,1,0:T(1,128)} %reshape.206), calls=%async_computation.2 | async-start | bytes 131072 | tf_op jit(solution)/shard_map/all_to_all | solution.py:62
  372.1 7.9 %all-to-all-done.2 = f32[64,1,160]{2,1,0:T(1,128)S(1)} async-done(((f32[64,1,160]{2,1,0:T(1,128)}), f32[64,1,160]{2,1,0:T(1,128)S(1)}, u32[]{:S(2)}, u32[]{:S(2)}) %all-to-all-start.2) | async-done | bytes 40992 | tf_op jit(solution)/shard_map/all_to_all | solution.py:62
  380.0 4.6 all-to-all-start.1
  384.7 2.2 copy.17
  386.9 6.6 all-to-all-done.1
  393.5 40.7 %all_to_all.20 = bf16[5,64,32,128]{3,2,0,1:T(8,128)(2,1)} all-to-all(bf16[5,64,32,128]{3,2,0,1:T(8,128)(2,1)S(1)} %copy.17), channel_id=1, replica_groups=mesh['seq'=64,'head'=8] {'seq'}, dimensions={1} | all-to-all | bytes 5242880 | tf_op jit(solution)/shard_map/all_to_all | solution.py:77
  434.2 3.2 stack.2
  437.4 5.8 all-to-all-start.3
  446.4 1.4 fusion.16
  448.9 1.3 fusion.15
  451.0 1.4 fusion.12
  452.6 98.9 %all-to-all-done.3 = bf16[64,640,80]{1,2,0:T(8,128)(2,1)} async-done(((bf16[64,640,80]{1,2,0:T(8,128)(2,1)}), bf16[64,640,80]{1,2,0:T(8,128)(2,1)}, u32[]{:S(2)}, u32[]{:S(2)}) %all-to-all-start.3) | async-done | bytes 6553632 | tf_op jit(solution)/shard_map/all_to_all | solution.py:45
  551.5 4.9 convolution_convert_fusion
  556.4 1.4 copy.25
  557.9 127.0 %reduce-scatter.4.cloned.1.call-done = bf16[640,32]{1,0:T(8,128)(2,1)} async-done(((bf16[5120,32]{1,0:T(8,128)(2,1)}), bf16[640,32]{1,0:T(8,128)(2,1)}) %reduce-scatter.4.cloned.1.call-update) | async-done | bytes 40976
  685.9 2.7 scatter_custom_fusion.1
  (68 shorter events, 17.9 us)
Async XLA Ops:
  6.5 679.4 %copy-start = (bf16[256,640]{1,0:T(8,128)(2,1)S(1)}, bf16[256,640]{1,0:T(8,128)(2,1)}, u32[]{:S(2)}) copy-start(bf16[256,640]{1,0:T(8,128)(2,1)} %param.12) | copy-start | bytes 983044
  6.5 330.0 %all-gather.3.cloned.1.call-start = ((), (), s32[]{:S(2)}) async-start(), calls=%async_computation.5 | async-start | bytes 2662400 | tf_op jit(solution)/shard_map/all_gather | solution.py:58
  14.8 2.3 copy-start.4
  362.2 22.4 %copy-start.2 = (bf16[5,2048,128]{2,1,0:T(8,128)(2,1)}, bf16[5,2048,128]{2,1,0:T(8,128)(2,1)S(1)}, u32[]{:S(2)}) copy-start(bf16[5,2048,128]{2,1,0:T(8,128)(2,1)S(1)} %get-tuple-element.49) | copy-start | bytes 7864324
  363.5 16.5 %all-to-all-start.2 = ((f32[64,1,160]{2,1,0:T(1,128)}), f32[64,1,160]{2,1,0:T(1,128)S(1)}, u32[]{:S(2)}, u32[]{:S(2)}) async-start(f32[64,1,160]{2,1,0:T(1,128)} %reshape.206), calls=%async_computation.2 | async-start | bytes 131072 | tf_op jit(solution)/shard_map/all_to_all | solution.py:62
  380.0 13.5 %all-to-all-start.1 = ((f32[64,1,160]{2,1,0:T(1,128)}), f32[64,1,160]{2,1,0:T(1,128)S(1)}, u32[]{:S(2)}, u32[]{:S(2)}) async-start(f32[64,1,160]{2,1,0:T(1,128)} %reshape.204), calls=%async_computation.1 | async-start | bytes 131072 | tf_op jit(solution)/shard_map/all_to_all | solution.py:69
  386.8 47.3 %copy-start.3 = (bf16[640,80]{0,1:T(8,128)(2,1)S(1)}, bf16[640,80]{0,1:T(8,128)(2,1)}, u32[]{:S(2)}) copy-start(bf16[640,80]{0,1:T(8,128)(2,1)} %param.15) | copy-start | bytes 307204
  437.4 13.6 %copy-start.1 = (bf16[5,64,32,128]{3,2,0,1:T(8,128)(2,1)S(1)}, bf16[5,64,32,128]{3,2,0,1:T(8,128)(2,1)}, u32[]{:S(2)}) copy-start(bf16[5,64,32,128]{3,2,0,1:T(8,128)(2,1)} %all_to_all.20) | copy-start | bytes 7864324
  437.4 114.1 %all-to-all-start.3 = ((bf16[64,640,80]{1,2,0:T(8,128)(2,1)}), bf16[64,640,80]{1,2,0:T(8,128)(2,1)}, u32[]{:S(2)}, u32[]{:S(2)}) async-start(bf16[64,640,80]{1,2,0:T(8,128)(2,1)} %stack.2), calls=%async_computation.3 | async-start | bytes 13107200 | tf_op jit(solution)/shard_map/all_to_all | solution.py:45
  443.2 241.6 %reduce-scatter.4.cloned.1.call-start = ((), (), s32[]{:S(2)}) async-start(), calls=%async_computation.6 | async-start | bytes 1474560
  556.4 129.5 %copy-start.5 = (s32[1024]{0:T(1024)S(1)}, s32[1024]{0:T(1024)}, u32[]{:S(2)}) copy-start(s32[1024]{0:T(1024)} %copy-done.4) | copy-start | bytes 12292
Sparse Core Ops, SparseCore 0:
  17.2 319.2 all-gather.2
  558.0 126.8 reduce-scatter.3
